TPU v7x, 32 devices: a whole 2x2x4 slice. The times are simulated.
32 devices in a mesh: grp: 2 (over y), tile: 4 (over z), date: 2 (over x), pol: 2 (over core).
Axes of the slice: x: 2, y: 2, z: 4, core: 2. Of those that a mesh axis runs over, the one named last changes fastest.
Arguments:
- stack: bfloat16 [2, 16, 3, 16384], P(None, ('date', 'pol'), None, ('grp', 'tile')), parts along dimension 3, may hold values from -40 to 40
- nbr_tile: int32 [16, 16384], P(None, ('grp', 'tile', 'date', 'pol')), parts along dimension 1, may hold values from 0 to 3, as said below
- nbr_slot: int32 [16, 16384], P(None, ('grp', 'tile', 'date', 'pol')), parts along dimension 1, may hold values from 0 to 511, as said below
- nbr_valid: int32 [16, 16384], P(None, ('grp', 'tile', 'date', 'pol')), parts along dimension 1, may hold values from 0 to 1
- fetch_rows: int32 [8, 4, 4, 128], P(('grp', 'tile'), ('date', 'pol')), parts along dimension 0, may hold values from 0 to 511
Outputs:
- linked: float32 [2, 16, 3, 16384], P(None, None, None, ('grp', 'tile', 'date', 'pol')), parts along dimension 3
There are 2 independent parts, one for each index of `grp`. A program takes and returns all parts, laid end to end along the dimension named above; each array names one. Nothing has to cross between parts.
Inputs may be any that keep to these rules, and one draw needn't show every extreme that they name: `nbr_tile`: entry 0 of every pixel names the pixel's own tile. `nbr_slot`: where nbr_tile is the pixel's own tile, a row of the pixel's own block, entry 0 being the pixel itself; elsewhere a slot of the fetch list of the pixel's block toward that tile.
All inputs are finite; a program needn't handle non-finite values.
Results may differ from a plain program's by a relative error of at most 0.0003.
Values may be sent and summed in bfloat16 or wider, within the bound.
A program may use at most 64 MiB of HBM per device.

v0:
```python
import math

import jax
import jax.numpy as jnp
from jax import lax
from jax.sharding import PartitionSpec as P

POWER_ITERS = 8


eps = 1e-06
floor_value = 0.3


def phase_link(gram, start_rows, channels):
    highest = lax.Precision.HIGHEST
    real_part = gram[:, :channels, :channels] + gram[:, channels:, channels:]
    cross = gram[:, :channels, channels:]
    imag_part = jnp.transpose(cross, (0, 2, 1)) - cross
    upper = jnp.concatenate([real_part, -imag_part], axis=2)
    lower = jnp.concatenate([imag_part, real_part], axis=2)
    operator = jnp.concatenate([upper, lower], axis=1)
    vector = start_rows
    for turn in range(POWER_ITERS):
        image = jnp.einsum("bij,bj->bi", operator, vector, precision=highest)
        factor = lax.rsqrt(jnp.sum(image * image, axis=1) / channels + eps)
        vector = image * factor[:, None]
    vec_real = vector[:, :channels]
    vec_imag = vector[:, channels:]
    first_real = vec_real[:, :1]
    first_imag = vec_imag[:, :1]
    denom = jnp.maximum(jnp.sqrt(first_real * first_real + first_imag * first_imag), floor_value)
    out_real = (vec_real * first_real + vec_imag * first_imag) / denom
    out_imag = (vec_imag * first_real - vec_real * first_imag) / denom
    return jnp.stack([out_real, out_imag], axis=1)


def body(stack, nbr_tile, nbr_slot, nbr_valid, fetch_rows):
    arrived = lax.all_to_all(stack, ("date", "pol"), split_axis=3, concat_axis=1, tiled=True)
    width = arrived.shape[3]
    features = arrived.shape[0] * arrived.shape[1] * arrived.shape[2]
    channels = features // 2
    rows_here = arrived.reshape(features, width).T
    tiles = lax.axis_size("tile")
    wanted = fetch_rows.reshape(tiles, -1)
    capacity = wanted.shape[1]
    owners = lax.broadcasted_iota(jnp.int32, (tiles, capacity), 0)
    wanted_all = (owners * width + wanted).reshape(-1)
    empty = jnp.zeros((tiles * capacity, features), jnp.bfloat16)
    piece = lax.all_gather(rows_here, "tile", axis=0, tiled=True)
    inside = (wanted_all >= 0) & (wanted_all < piece.shape[0])
    picked = jnp.take(piece, jnp.clip(wanted_all, 0, piece.shape[0] - 1), axis=0)
    fetched = jnp.where(inside[:, None], picked, empty)
    table = jnp.concatenate([rows_here, fetched], axis=0)
    own_tile = lax.axis_index("tile")
    source = jnp.where(nbr_tile == own_tile, nbr_slot, width + nbr_tile * capacity + nbr_slot)
    weights = nbr_valid.astype(jnp.bfloat16)
    block = math.gcd(width, 128)

    def link_block(number):
        begin = number * block
        chosen = lax.dynamic_slice_in_dim(source, begin, block, 1).T
        keep = lax.dynamic_slice_in_dim(weights, begin, block, 1).T
        start_rows = lax.dynamic_slice_in_dim(rows_here, begin, block, 0).astype(jnp.float32)
        near = jnp.take(table, chosen, axis=0) * keep[:, :, None]
        gram = jnp.einsum("bkf,bkg->bfg", near, near, preferred_element_type=jnp.float32)
        return phase_link(gram, start_rows, channels)

    linked = lax.map(link_block, jnp.arange(width // block, dtype=jnp.int32))
    linked = jnp.transpose(linked.reshape(width, 2, channels), (1, 2, 0))
    return linked.reshape(arrived.shape[0], arrived.shape[1], arrived.shape[2], width)


def solution(mesh):
    in_specs = (
        P(None, ("date", "pol"), None, ("grp", "tile")),
        P(None, ("grp", "tile", "date", "pol")),
        P(None, ("grp", "tile", "date", "pol")),
        P(None, ("grp", "tile", "date", "pol")),
        P(("grp", "tile"), ("date", "pol"), None, None),
    )
    out_specs = P(None, None, None, ("grp", "tile", "date", "pol"))
    return jax.shard_map(body, mesh=mesh, in_specs=in_specs, out_specs=out_specs, check_vma=False)
```

profile of v0, /device:TPU:0, one launch (start us, length us, event | category | flops | bytes accessed | tf_op | source)
XLA Modules:
  0.0 344.1 jit_solution(6011919794856671223)
XLA Ops:
  0.0 6.0 %copy.61 = bf16[2,4,3,2048]{1,2,0,3:T(4,128)(2,1)} copy(bf16[2,4,3,2048]{3,1,2,0:T(4,128)(2,1)} %param.7) | data formatting | bytes 196608 | tf_op args[0]
  6.0 5.9 %reshape.151 = bf16[4,2,6144]{2,1,0:T(2,128)(2,1)} reshape(bf16[2048,2,3,4]{3,2,1,0:T(4,128)(2,1)} %bitcast.122) | data formatting | bytes 196608
  11.9 4.2 %all-to-all-start = ((bf16[4,2,6144]{2,1,0:T(2,128)(2,1)}), bf16[4,2,6144]{2,1,0:T(2,128)(2,1)S(1)}, u32[]{:S(2)}, u32[]{:S(2)}) async-start(bf16[4,2,6144]{2,1,0:T(2,128)(2,1)} %reshape.151), calls=%async_computation | async-start | bytes 196608 | tf_op jit(solution)/shard_map/all_to_all | solution.py:39
  20.4 4.7 %reshape.152 = bf16[2048,2,3,4]{3,2,1,0:T(4,128)(2,1)} reshape(bf16[4,2,6144]{2,1,0:T(2,128)(2,1)S(1)} %all-to-all-done) | data formatting | bytes 196608
  25.2 6.1 %copy.62 = bf16[2,4,3,4,512]{4,2,1,3,0:T(4,128)(2,1)S(1)} copy(bf16[2,4,3,4,512]{1,2,0,4,3:T(4,128)(2,1)} %bitcast.121) | data formatting | bytes 196608 | tf_op jit(solution)/shard_map/all_to_all | solution.py:39
  31.6 16.3 %all_gather.3 = bf16[2048,96]{1,0:T(8,128)(2,1)S(1)} all-gather(bf16[512,96]{1,0:T(8,128)(2,1)S(1)} %bitcast.124), channel_id=1, replica_groups=mesh['grp'=2,'tile'=4,'date'=2,'pol'=2] {'tile'}, dimensions={0}, use_global_device_ids=true | all-gather | bytes 491520 | tf_op jit(solution)/shard_map/all_gather | solution.py:50
  49.5 292.7 %while.10 = (s32[]{:T(128)}, f32[4,128,2,48]{1,0,3,2:T(4,128)}, s32[4]{0:T(128)S(1)}, s32[16,512]{1,0:T(8,128)S(1)}, bf16[1024,96]{1,0:T(8,128)(2,1)S(1)}, /*ind...) while((s32[]{:T(128)}, f32[4,128,2,48]{1,0,3,2:T(4,128)}, ...), condition=%wide.region_9.10_spmd, body=%wide.region_0.9_spmd.sunk | while | flops 73528832 | bytes 106918248 | solution.py:69
  51.3 6.2 %gather_fusion = bf16[2048,96]{1,0:T(8,128)(2,1)S(1)} fusion(bf16[1024,96]{1,0:T(8,128)(2,1)S(1)} %get-tuple-element.159, s32[2048]{0:T(1024)S(1)} %broadcast_clamp_fusion.2), kind=kCustom, calls=%fused_computation.clone.1 | custom fusion | bytes 794624 | tf_op jit(solution)/shard_map/while/body/eval_jaxpr/jit(_take)/gather | solution.py:65
  67.6 6.4 %fusion.35 = (f32[128,48,48]{2,1,0:T(8,128)S(1)}, f32[128,48,48]{2,1,0:T(8,128)S(1)}, f32[128,48,48]{2,1,0:T(8,128)S(1)}) fusion(f32[128,96,96]{2,1,0:T(8,128)} %copy-done.1, f32[128,48,48]{1,2,0:T(8,128)} %copy.138), kind=kLoop, calls=%fused_computation.74.clone.1 | loop fusion | flops 884736 | bytes 8257536 | tf_op jit(solution)/shard_map/while/body/eval_jaxpr/neg | solution.py:20
  78.8 5.0 %fusion.36 = f32[128,1,96]{2,1,0:T(1,128)S(1)} fusion(f32[128,96,96]{2,1,0:T(8,128)S(1)} %maximum_maximum_fusion.2, bf16[128,96,1]{1,0,2:T(8,128)(2,1)S(1)} %dynamic-slice_bitcast_fusion.5), kind=kOutput, calls=%fused_computation.25.clone.1 | convolution fusion | flops 14155776 | bytes 4792320 | tf_op jit(solution)/shard_map/while/body/eval_jaxpr/bij,bj->bi/dot_general | solution.py:25
  84.1 5.0 %fusion.38 = f32[128,96]{1,0:T(8,128)S(1)} fusion(f32[128,96,96]{2,1,0:T(8,128)} %copy-done, f32[128,96]{1,0:T(8,128)S(1)} %copy.140), kind=kLoop, calls=%fused_computation.15.clone.1 | loop fusion | flops 2347008 | bytes 4816896 | tf_op jit(solution)/shard_map/while
  89.4 5.0 %fusion.39 = f32[128,96]{1,0:T(8,128)S(1)} fusion(f32[128,96,96]{2,1,0:T(8,128)} %copy-done, f32[128,96]{1,0:T(8,128)S(1)} %copy.142), kind=kLoop, calls=%fused_computation.14.clone.1 | loop fusion | flops 2347008 | bytes 4816896 | tf_op jit(solution)/shard_map/while
  94.6 5.0 %fusion.40 = f32[128,96]{1,0:T(8,128)S(1)} fusion(f32[128,96,96]{2,1,0:T(8,128)} %copy-done, f32[128,96]{1,0:T(8,128)S(1)} %copy.144), kind=kLoop, calls=%fused_computation.13.clone.1 | loop fusion | flops 2347008 | bytes 4816896 | tf_op jit(solution)/shard_map/while
  99.9 5.0 %fusion.41 = f32[128,96]{1,0:T(8,128)S(1)} fusion(f32[128,96,96]{2,1,0:T(8,128)} %copy-done, f32[128,96]{1,0:T(8,128)S(1)} %copy.146), kind=kLoop, calls=%fused_computation.12.clone.1 | loop fusion | flops 2347008 | bytes 4816896 | tf_op jit(solution)/shard_map/while
  105.2 5.0 %fusion.42 = f32[128,96]{1,0:T(8,128)S(1)} fusion(f32[128,96,96]{2,1,0:T(8,128)} %copy-done, f32[128,96]{1,0:T(8,128)S(1)} %copy.148), kind=kLoop, calls=%fused_computation.11.clone.1 | loop fusion | flops 2347008 | bytes 4816896 | tf_op jit(solution)/shard_map/while
  110.5 5.1 %fusion.43 = f32[128,96]{1,0:T(8,128)S(1)} fusion(f32[128,96,96]{2,1,0:T(8,128)} %copy-done, f32[128,96]{1,0:T(8,128)S(1)} %copy.150), kind=kLoop, calls=%fused_computation.10.clone.1 | loop fusion | flops 2347008 | bytes 4816896 | tf_op jit(solution)/shard_map/while
  115.8 5.0 %multiply_reduce_fusion.22 = f32[128,96]{1,0:T(8,128)S(1)} fusion(f32[128,96,96]{2,1,0:T(8,128)} %copy-done, f32[128,96]{1,0:T(8,128)S(1)} %copy.152), kind=kLoop, calls=%fused_computation.3.clone.1 | loop fusion | flops 2347008 | bytes 4816896 | tf_op jit(solution)/shard_map/while
  124.4 6.2 %gather_fusion = bf16[2048,96]{1,0:T(8,128)(2,1)S(1)} fusion(bf16[1024,96]{1,0:T(8,128)(2,1)S(1)} %get-tuple-element.159, s32[2048]{0:T(1024)S(1)} %broadcast_clamp_fusion.2), kind=kCustom, calls=%fused_computation.clone.1 | custom fusion | bytes 794624 | tf_op jit(solution)/shard_map/while/body/eval_jaxpr/jit(_take)/gather | solution.py:65
  140.7 6.4 %fusion.35 = (f32[128,48,48]{2,1,0:T(8,128)S(1)}, f32[128,48,48]{2,1,0:T(8,128)S(1)}, f32[128,48,48]{2,1,0:T(8,128)S(1)}) fusion(f32[128,96,96]{2,1,0:T(8,128)} %copy-done.1, f32[128,48,48]{1,2,0:T(8,128)} %copy.138), kind=kLoop, calls=%fused_computation.74.clone.1 | loop fusion | flops 884736 | bytes 8257536 | tf_op jit(solution)/shard_map/while/body/eval_jaxpr/neg | solution.py:20
  152.0 5.0 %fusion.36 = f32[128,1,96]{2,1,0:T(1,128)S(1)} fusion(f32[128,96,96]{2,1,0:T(8,128)S(1)} %maximum_maximum_fusion.2, bf16[128,96,1]{1,0,2:T(8,128)(2,1)S(1)} %dynamic-slice_bitcast_fusion.5), kind=kOutput, calls=%fused_computation.25.clone.1 | convolution fusion | flops 14155776 | bytes 4792320 | tf_op jit(solution)/shard_map/while/body/eval_jaxpr/bij,bj->bi/dot_general | solution.py:25
  157.2 5.0 %fusion.38 = f32[128,96]{1,0:T(8,128)S(1)} fusion(f32[128,96,96]{2,1,0:T(8,128)} %copy-done, f32[128,96]{1,0:T(8,128)S(1)} %copy.140), kind=kLoop, calls=%fused_computation.15.clone.1 | loop fusion | flops 2347008 | bytes 4816896 | tf_op jit(solution)/shard_map/while
  162.5 5.0 %fusion.39 = f32[128,96]{1,0:T(8,128)S(1)} fusion(f32[128,96,96]{2,1,0:T(8,128)} %copy-done, f32[128,96]{1,0:T(8,128)S(1)} %copy.142), kind=kLoop, calls=%fused_computation.14.clone.1 | loop fusion | flops 2347008 | bytes 4816896 | tf_op jit(solution)/shard_map/while
  167.8 5.0 %fusion.40 = f32[128,96]{1,0:T(8,128)S(1)} fusion(f32[128,96,96]{2,1,0:T(8,128)} %copy-done, f32[128,96]{1,0:T(8,128)S(1)} %copy.144), kind=kLoop, calls=%fused_computation.13.clone.1 | loop fusion | flops 2347008 | bytes 4816896 | tf_op jit(solution)/shard_map/while
  173.0 5.0 %fusion.41 = f32[128,96]{1,0:T(8,128)S(1)} fusion(f32[128,96,96]{2,1,0:T(8,128)} %copy-done, f32[128,96]{1,0:T(8,128)S(1)} %copy.146), kind=kLoop, calls=%fused_computation.12.clone.1 | loop fusion | flops 2347008 | bytes 4816896 | tf_op jit(solution)/shard_map/while
  178.3 5.0 %fusion.42 = f32[128,96]{1,0:T(8,128)S(1)} fusion(f32[128,96,96]{2,1,0:T(8,128)} %copy-done, f32[128,96]{1,0:T(8,128)S(1)} %copy.148), kind=kLoop, calls=%fused_computation.11.clone.1 | loop fusion | flops 2347008 | bytes 4816896 | tf_op jit(solution)/shard_map/while
  183.6 5.1 %fusion.43 = f32[128,96]{1,0:T(8,128)S(1)} fusion(f32[128,96,96]{2,1,0:T(8,128)} %copy-done, f32[128,96]{1,0:T(8,128)S(1)} %copy.150), kind=kLoop, calls=%fused_computation.10.clone.1 | loop fusion | flops 2347008 | bytes 4816896 | tf_op jit(solution)/shard_map/while
  188.9 5.0 %multiply_reduce_fusion.22 = f32[128,96]{1,0:T(8,128)S(1)} fusion(f32[128,96,96]{2,1,0:T(8,128)} %copy-done, f32[128,96]{1,0:T(8,128)S(1)} %copy.152), kind=kLoop, calls=%fused_computation.3.clone.1 | loop fusion | flops 2347008 | bytes 4816896 | tf_op jit(solution)/shard_map/while
  197.5 6.2 %gather_fusion = bf16[2048,96]{1,0:T(8,128)(2,1)S(1)} fusion(bf16[1024,96]{1,0:T(8,128)(2,1)S(1)} %get-tuple-element.159, s32[2048]{0:T(1024)S(1)} %broadcast_clamp_fusion.2), kind=kCustom, calls=%fused_computation.clone.1 | custom fusion | bytes 794624 | tf_op jit(solution)/shard_map/while/body/eval_jaxpr/jit(_take)/gather | solution.py:65
  203.8 4.1 %fusion.34 = f32[128,96,96]{2,1,0:T(8,128)S(1)} fusion(bf16[128,16,96]{2,1,0:T(8,128)(2,1)S(1)} %bitcast.120, pred[128,16]{1,0:T(8,128)(4,1)S(1)} %compare_and_fusion.4, bf16[128,16]{1,0:T(8,128)(2,1)S(1)} %dynamic-slice_bitcast_fusion.4), kind=kOutput, calls=%fused_computation.18.clone.1 | convolution fusion | flops 38141952 | bytes 5117952 | tf_op jit(solution)/shard_map/while/body/eval_jaxpr/bkf,bkg->bfg/dot_general | solution.py:66
  213.9 6.4 %fusion.35 = (f32[128,48,48]{2,1,0:T(8,128)S(1)}, f32[128,48,48]{2,1,0:T(8,128)S(1)}, f32[128,48,48]{2,1,0:T(8,128)S(1)}) fusion(f32[128,96,96]{2,1,0:T(8,128)} %copy-done.1, f32[128,48,48]{1,2,0:T(8,128)} %copy.138), kind=kLoop, calls=%fused_computation.74.clone.1 | loop fusion | flops 884736 | bytes 8257536 | tf_op jit(solution)/shard_map/while/body/eval_jaxpr/neg | solution.py:20
  225.1 5.0 %fusion.36 = f32[128,1,96]{2,1,0:T(1,128)S(1)} fusion(f32[128,96,96]{2,1,0:T(8,128)S(1)} %maximum_maximum_fusion.2, bf16[128,96,1]{1,0,2:T(8,128)(2,1)S(1)} %dynamic-slice_bitcast_fusion.5), kind=kOutput, calls=%fused_computation.25.clone.1 | convolution fusion | flops 14155776 | bytes 4792320 | tf_op jit(solution)/shard_map/while/body/eval_jaxpr/bij,bj->bi/dot_general | solution.py:25
  230.3 5.0 %fusion.38 = f32[128,96]{1,0:T(8,128)S(1)} fusion(f32[128,96,96]{2,1,0:T(8,128)} %copy-done, f32[128,96]{1,0:T(8,128)S(1)} %copy.140), kind=kLoop, calls=%fused_computation.15.clone.1 | loop fusion | flops 2347008 | bytes 4816896 | tf_op jit(solution)/shard_map/while
  235.6 5.0 %fusion.39 = f32[128,96]{1,0:T(8,128)S(1)} fusion(f32[128,96,96]{2,1,0:T(8,128)} %copy-done, f32[128,96]{1,0:T(8,128)S(1)} %copy.142), kind=kLoop, calls=%fused_computation.14.clone.1 | loop fusion | flops 2347008 | bytes 4816896 | tf_op jit(solution)/shard_map/while
  240.9 5.0 %fusion.40 = f32[128,96]{1,0:T(8,128)S(1)} fusion(f32[128,96,96]{2,1,0:T(8,128)} %copy-done, f32[128,96]{1,0:T(8,128)S(1)} %copy.144), kind=kLoop, calls=%fused_computation.13.clone.1 | loop fusion | flops 2347008 | bytes 4816896 | tf_op jit(solution)/shard_map/while
  246.2 5.0 %fusion.41 = f32[128,96]{1,0:T(8,128)S(1)} fusion(f32[128,96,96]{2,1,0:T(8,128)} %copy-done, f32[128,96]{1,0:T(8,128)S(1)} %copy.146), kind=kLoop, calls=%fused_computation.12.clone.1 | loop fusion | flops 2347008 | bytes 4816896 | tf_op jit(solution)/shard_map/while
  251.4 5.0 %fusion.42 = f32[128,96]{1,0:T(8,128)S(1)} fusion(f32[128,96,96]{2,1,0:T(8,128)} %copy-done, f32[128,96]{1,0:T(8,128)S(1)} %copy.148), kind=kLoop, calls=%fused_computation.11.clone.1 | loop fusion | flops 2347008 | bytes 4816896 | tf_op jit(solution)/shard_map/while
  256.7 5.1 %fusion.43 = f32[128,96]{1,0:T(8,128)S(1)} fusion(f32[128,96,96]{2,1,0:T(8,128)} %copy-done, f32[128,96]{1,0:T(8,128)S(1)} %copy.150), kind=kLoop, calls=%fused_computation.10.clone.1 | loop fusion | flops 2347008 | bytes 4816896 | tf_op jit(solution)/shard_map/while
  262.0 5.0 %multiply_reduce_fusion.22 = f32[128,96]{1,0:T(8,128)S(1)} fusion(f32[128,96,96]{2,1,0:T(8,128)} %copy-done, f32[128,96]{1,0:T(8,128)S(1)} %copy.152), kind=kLoop, calls=%fused_computation.3.clone.1 | loop fusion | flops 2347008 | bytes 4816896 | tf_op jit(solution)/shard_map/while
  270.7 6.2 %gather_fusion = bf16[2048,96]{1,0:T(8,128)(2,1)S(1)} fusion(bf16[1024,96]{1,0:T(8,128)(2,1)S(1)} %get-tuple-element.159, s32[2048]{0:T(1024)S(1)} %broadcast_clamp_fusion.2), kind=kCustom, calls=%fused_computation.clone.1 | custom fusion | bytes 794624 | tf_op jit(solution)/shard_map/while/body/eval_jaxpr/jit(_take)/gather | solution.py:65
  287.0 6.4 %fusion.35 = (f32[128,48,48]{2,1,0:T(8,128)S(1)}, f32[128,48,48]{2,1,0:T(8,128)S(1)}, f32[128,48,48]{2,1,0:T(8,128)S(1)}) fusion(f32[128,96,96]{2,1,0:T(8,128)} %copy-done.1, f32[128,48,48]{1,2,0:T(8,128)} %copy.138), kind=kLoop, calls=%fused_computation.74.clone.1 | loop fusion | flops 884736 | bytes 8257536 | tf_op jit(solution)/shard_map/while/body/eval_jaxpr/neg | solution.py:20
  298.2 5.0 %fusion.36 = f32[128,1,96]{2,1,0:T(1,128)S(1)} fusion(f32[128,96,96]{2,1,0:T(8,128)S(1)} %maximum_maximum_fusion.2, bf16[128,96,1]{1,0,2:T(8,128)(2,1)S(1)} %dynamic-slice_bitcast_fusion.5), kind=kOutput, calls=%fused_computation.25.clone.1 | convolution fusion | flops 14155776 | bytes 4792320 | tf_op jit(solution)/shard_map/while/body/eval_jaxpr/bij,bj->bi/dot_general | solution.py:25
  303.5 5.0 %fusion.38 = f32[128,96]{1,0:T(8,128)S(1)} fusion(f32[128,96,96]{2,1,0:T(8,128)} %copy-done, f32[128,96]{1,0:T(8,128)S(1)} %copy.140), kind=kLoop, calls=%fused_computation.15.clone.1 | loop fusion | flops 2347008 | bytes 4816896 | tf_op jit(solution)/shard_map/while
  308.7 5.0 %fusion.39 = f32[128,96]{1,0:T(8,128)S(1)} fusion(f32[128,96,96]{2,1,0:T(8,128)} %copy-done, f32[128,96]{1,0:T(8,128)S(1)} %copy.142), kind=kLoop, calls=%fused_computation.14.clone.1 | loop fusion | flops 2347008 | bytes 4816896 | tf_op jit(solution)/shard_map/while
  314.0 5.0 %fusion.40 = f32[128,96]{1,0:T(8,128)S(1)} fusion(f32[128,96,96]{2,1,0:T(8,128)} %copy-done, f32[128,96]{1,0:T(8,128)S(1)} %copy.144), kind=kLoop, calls=%fused_computation.13.clone.1 | loop fusion | flops 2347008 | bytes 4816896 | tf_op jit(solution)/shard_map/while
  319.3 5.0 %fusion.41 = f32[128,96]{1,0:T(8,128)S(1)} fusion(f32[128,96,96]{2,1,0:T(8,128)} %copy-done, f32[128,96]{1,0:T(8,128)S(1)} %copy.146), kind=kLoop, calls=%fused_computation.12.clone.1 | loop fusion | flops 2347008 | bytes 4816896 | tf_op jit(solution)/shard_map/while
  324.6 5.0 %fusion.42 = f32[128,96]{1,0:T(8,128)S(1)} fusion(f32[128,96,96]{2,1,0:T(8,128)} %copy-done, f32[128,96]{1,0:T(8,128)S(1)} %copy.148), kind=kLoop, calls=%fused_computation.11.clone.1 | loop fusion | flops 2347008 | bytes 4816896 | tf_op jit(solution)/shard_map/while
  329.9 5.1 %fusion.43 = f32[128,96]{1,0:T(8,128)S(1)} fusion(f32[128,96,96]{2,1,0:T(8,128)} %copy-done, f32[128,96]{1,0:T(8,128)S(1)} %copy.150), kind=kLoop, calls=%fused_computation.10.clone.1 | loop fusion | flops 2347008 | bytes 4816896 | tf_op jit(solution)/shard_map/while
  335.2 5.0 %multiply_reduce_fusion.22 = f32[128,96]{1,0:T(8,128)S(1)} fusion(f32[128,96,96]{2,1,0:T(8,128)} %copy-done, f32[128,96]{1,0:T(8,128)S(1)} %copy.152), kind=kLoop, calls=%fused_computation.3.clone.1 | loop fusion | flops 2347008 | bytes 4816896 | tf_op jit(solution)/shard_map/while
  (298 shorter events, 81.3 us)
Async XLA Ops:
  0.0 16.2 %copy-start.6 = (s32[16,512]{1,0:T(8,128)S(1)}, s32[16,512]{1,0:T(8,128)}, u32[]{:S(2)}) copy-start(s32[16,512]{1,0:T(8,128)} %param.10) | copy-start | bytes 98308
  0.0 16.3 %copy-start.9 = (s32[1,1,4,128]{3,2,1,0:T(4,128)S(1)}, s32[1,1,4,128]{3,2,1,0:T(4,128)}, u32[]{:S(2)}) copy-start(s32[1,1,4,128]{3,2,1,0:T(4,128)} %param.11) | copy-start | bytes 6148
  0.0 16.5 %copy-start.8 = (s32[16,512]{1,0:T(8,128)S(1)}, s32[16,512]{1,0:T(8,128)}, u32[]{:S(2)}) copy-start(s32[16,512]{1,0:T(8,128)} %param.8) | copy-start | bytes 98308
  0.0 16.5 %copy-start.7 = (s32[16,512]{1,0:T(8,128)S(1)}, s32[16,512]{1,0:T(8,128)}, u32[]{:S(2)}) copy-start(s32[16,512]{1,0:T(8,128)} %param.9) | copy-start | bytes 98308
  11.9 8.5 %all-to-all-start = ((bf16[4,2,6144]{2,1,0:T(2,128)(2,1)}), bf16[4,2,6144]{2,1,0:T(2,128)(2,1)S(1)}, u32[]{:S(2)}, u32[]{:S(2)}) async-start(bf16[4,2,6144]{2,1,0:T(2,128)(2,1)} %reshape.151), calls=%async_computation | async-start | bytes 196608 | tf_op jit(solution)/shard_map/all_to_all | solution.py:39
  49.7 1.4 copy-start.4
  49.7 7.8 %copy-start.2 = (bf16[16,512]{0,1:T(8,128)(2,1)}, bf16[16,512]{0,1:T(8,128)(2,1)S(1)}, u32[]{:S(2)}) copy-start(bf16[16,512]{0,1:T(8,128)(2,1)S(1)} %get-tuple-element.160) | copy-start | bytes 49156 | tf_op jit(solution)/shard_map/while
  61.7 2.7 copy-start.1
  76.2 2.7 copy-start
  110.5 12.4 %copy-start.3 = (bf16[16,512]{0,1:T(8,128)(2,1)S(1)}, bf16[16,512]{0,1:T(8,128)(2,1)}, u32[]{:S(2)}) copy-start(bf16[16,512]{0,1:T(8,128)(2,1)} %copy-done.2) | copy-start | bytes 49156 | tf_op jit(solution)/shard_map/while
  110.5 12.3 %copy-start.5 = (s32[16,512]{1,0:T(8,128)S(1)}, s32[16,512]{1,0:T(8,128)}, u32[]{:S(2)}) copy-start(s32[16,512]{1,0:T(8,128)} %copy-done.4) | copy-start | bytes 98308 | tf_op jit(solution)/shard_map/while
  122.8 1.4 copy-start.4
  122.8 7.8 %copy-start.2 = (bf16[16,512]{0,1:T(8,128)(2,1)}, bf16[16,512]{0,1:T(8,128)(2,1)S(1)}, u32[]{:S(2)}) copy-start(bf16[16,512]{0,1:T(8,128)(2,1)S(1)} %get-tuple-element.160) | copy-start | bytes 49156 | tf_op jit(solution)/shard_map/while
  134.8 2.7 copy-start.1
  149.3 2.7 copy-start
  183.6 12.4 %copy-start.3 = (bf16[16,512]{0,1:T(8,128)(2,1)S(1)}, bf16[16,512]{0,1:T(8,128)(2,1)}, u32[]{:S(2)}) copy-start(bf16[16,512]{0,1:T(8,128)(2,1)} %copy-done.2) | copy-start | bytes 49156 | tf_op jit(solution)/shard_map/while
  183.6 12.3 %copy-start.5 = (s32[16,512]{1,0:T(8,128)S(1)}, s32[16,512]{1,0:T(8,128)}, u32[]{:S(2)}) copy-start(s32[16,512]{1,0:T(8,128)} %copy-done.4) | copy-start | bytes 98308 | tf_op jit(solution)/shard_map/while
  195.9 1.4 copy-start.4
  195.9 7.8 %copy-start.2 = (bf16[16,512]{0,1:T(8,128)(2,1)}, bf16[16,512]{0,1:T(8,128)(2,1)S(1)}, u32[]{:S(2)}) copy-start(bf16[16,512]{0,1:T(8,128)(2,1)S(1)} %get-tuple-element.160) | copy-start | bytes 49156 | tf_op jit(solution)/shard_map/while
  207.9 2.7 copy-start.1
  222.4 2.7 copy-start
  256.7 12.4 %copy-start.3 = (bf16[16,512]{0,1:T(8,128)(2,1)S(1)}, bf16[16,512]{0,1:T(8,128)(2,1)}, u32[]{:S(2)}) copy-start(bf16[16,512]{0,1:T(8,128)(2,1)} %copy-done.2) | copy-start | bytes 49156 | tf_op jit(solution)/shard_map/while
  256.7 12.3 %copy-start.5 = (s32[16,512]{1,0:T(8,128)S(1)}, s32[16,512]{1,0:T(8,128)}, u32[]{:S(2)}) copy-start(s32[16,512]{1,0:T(8,128)} %copy-done.4) | copy-start | bytes 98308 | tf_op jit(solution)/shard_map/while
  269.1 1.4 copy-start.4
  269.1 7.8 %copy-start.2 = (bf16[16,512]{0,1:T(8,128)(2,1)}, bf16[16,512]{0,1:T(8,128)(2,1)S(1)}, u32[]{:S(2)}) copy-start(bf16[16,512]{0,1:T(8,128)(2,1)S(1)} %get-tuple-element.160) | copy-start | bytes 49156 | tf_op jit(solution)/shard_map/while
  281.1 2.7 copy-start.1
  295.6 2.7 copy-start
  329.8 12.4 %copy-start.3 = (bf16[16,512]{0,1:T(8,128)(2,1)S(1)}, bf16[16,512]{0,1:T(8,128)(2,1)}, u32[]{:S(2)}) copy-start(bf16[16,512]{0,1:T(8,128)(2,1)} %copy-done.2) | copy-start | bytes 49156 | tf_op jit(solution)/shard_map/while
  329.9 12.3 %copy-start.5 = (s32[16,512]{1,0:T(8,128)S(1)}, s32[16,512]{1,0:T(8,128)}, u32[]{:S(2)}) copy-start(s32[16,512]{1,0:T(8,128)} %copy-done.4) | copy-start | bytes 98308 | tf_op jit(solution)/shard_map/while
where the time goes:
time: 346 us; the launch traced here: 344 us
  other arithmetic  177 us (51%)
  local copies, waits for them, and re-layouts  102 us (29%)
  matrix products  36.4 us (11%)
  blocking collectives  16.3 us (5%)
  loops' own time  4.38 us (1%)
  starting transfers between devices  4.23 us (1%)
  waiting for transfers between devices  3.91 us (1%)
    while x28, other arithmetic  141 us
    neg x4, other arithmetic, phase_link(): upper = jnp.concatenate([real_part, -imag_part], axis=2)  25.4 us
    gather x4, local copies, waits for them, and re-layouts, link_block(): near = jnp.take(table, chosen, axis=0) * keep[:, :, None]  24.7 us
    while x76, local copies, waits for them, and re-layouts  23.9 us
    dot_general x4, matrix products, phase_link(): image = jnp.einsum('bij,bj->bi', operator, vector, precision=highest)  19.9 us
    unnamed x12, local copies, waits for them, and re-layouts  16.8 us
    dot_general x4, matrix products, link_block(): jnp.einsum('bkf,bkg->bfg', near, near, preferred_element_type=jnp.float32)  16.5 us
    all_gather x1, blocking collectives, body(): piece = lax.all_gather(rows_here, 'tile', axis=0, tiled=True)  16.3 us
  transfers between devices with their start and end apart: 1, of which 1 were waited for; matrix products, arithmetic and copies ran while one was open for 0% of the time, Pallas kernels for 0%

commit v1 on v0

v1 whole, which is shorter than its diff:
```python
import functools

import jax
import jax.numpy as jnp
from jax import lax
from jax.experimental import pallas as pl
from jax.experimental.pallas import tpu as pltpu
from jax.sharding import PartitionSpec as P

POWER_ITERS = 8
LANES = 128
PIECE = 256
MESH = pl.DeviceIdType.MESH

eps = 1e-06
floor_value = 0.3


def one_hot(index, rows):
    row = lax.broadcasted_iota(jnp.int32, (rows, index.shape[1]), 0)
    return jnp.where(row == index, 1.0, 0.0).astype(jnp.bfloat16)


def gather_kernel(dates, pols, tiles, stack_ref, wanted_ref, table_ref, fetched_ref,
                  outbox, inbox, asked, picked,
                  out_sem, in_sem, ask_sem, asked_sem, pick_sem, fetch_sem):
    strips = dates * pols
    parts, sets, local, _ = stack_ref.shape
    rows = parts * sets * local
    width = table_ref.shape[1]
    capacity = wanted_ref.shape[-1]
    date, pol, tile = lax.axis_index("date"), lax.axis_index("pol"), lax.axis_index("tile")
    me = date * pols + pol

    barrier = pltpu.get_barrier_semaphore()
    for step in range(1, strips):
        peer = lax.rem(me + step, strips)
        pl.semaphore_signal(barrier, inc=1, device_id={"date": peer // pols, "pol": lax.rem(peer, pols)},
                            device_id_type=MESH)
    for step in range(1, tiles):
        pl.semaphore_signal(barrier, inc=1, device_id={"tile": lax.rem(tile + step, tiles)}, device_id_type=MESH)

    pieces = [stack_ref[r, p].astype(jnp.float32) for r in range(parts) for p in range(sets)]
    fill = outbox.shape[1] - rows
    pieces.append(jnp.zeros((fill, stack_ref.shape[3]), jnp.float32))
    ready = jnp.concatenate(pieces, axis=0).astype(jnp.bfloat16)
    for s in range(strips):
        outbox[s] = ready[:, s * width:(s + 1) * width]

    pl.semaphore_wait(barrier, strips - 1 + tiles - 1)

    asks = []
    for step in range(1, tiles):
        peer = lax.rem(tile + step, tiles)
        copy = pltpu.make_async_remote_copy(
            src_ref=wanted_ref.at[peer], dst_ref=asked.at[step],
            send_sem=ask_sem.at[step], recv_sem=asked_sem.at[step],
            device_id={"tile": peer}, device_id_type=MESH)
        copy.start()
        asks.append(copy)
    sends = []
    for step in range(1, strips):
        peer = lax.rem(me + step, strips)
        copy = pltpu.make_async_remote_copy(
            src_ref=outbox.at[peer], dst_ref=inbox.at[me],
            send_sem=out_sem.at[step], recv_sem=in_sem.at[step],
            device_id={"date": peer // pols, "pol": lax.rem(peer, pols)}, device_id_type=MESH)
        copy.start()
        sends.append(copy)
    inbox[me] = outbox[me]
    fetched_ref[tile] = jnp.zeros(fetched_ref.shape[1:], jnp.bfloat16)
    for copy in sends:
        copy.wait_recv()

    arrived = [inbox[s].astype(jnp.float32) for s in range(strips)]
    pieces = []
    for group in range(parts * sets):
        for s in range(strips):
            pieces.append(arrived[s][group * local:(group + 1) * local])
    table = jnp.concatenate(pieces, axis=0).astype(jnp.bfloat16)
    table_ref[...] = table

    picks = []
    for step in range(1, tiles):
        asks[step - 1].wait_recv()
        asker = lax.rem(tile + tiles - step, tiles)
        chosen = jnp.dot(table, one_hot(asked[step], width), preferred_element_type=jnp.float32)
        picked[step] = chosen.astype(jnp.bfloat16)
        copy = pltpu.make_async_remote_copy(
            src_ref=picked.at[step], dst_ref=fetched_ref.at[tile],
            send_sem=pick_sem.at[step], recv_sem=fetch_sem.at[step],
            device_id={"tile": asker}, device_id_type=MESH)
        copy.start()
        picks.append(copy)
    for copy in picks:
        copy.wait_recv()
    for copy in asks + sends + picks:
        copy.wait_send()


def link_kernel(home_ref, table_ref, fetched_ref, tile_ref, slot_ref, valid_ref, out_ref,
                rows_ref, source_ref, near_ref, gram_re, gram_im):
    features, width = table_ref.shape
    tiles, _, capacity = fetched_ref.shape
    channels = features // 2
    neigh = tile_ref.shape[0]
    chunks = width // LANES
    half = channels // 8
    total = rows_ref.shape[1]

    rows_ref[:, :width] = table_ref[...]
    for q in range(tiles):
        rows_ref[:, width + q * capacity:width + (q + 1) * capacity] = fetched_ref[q]
    owner = tile_ref[...]
    slot = slot_ref[...]
    source_ref[...] = jnp.where(owner == home_ref[0], slot, width + owner * capacity + slot)

    def fetch(k, carry):
        index = source_ref[pl.ds(k, 1), :]
        near = jnp.zeros((features, width), jnp.float32)
        for begin in range(0, total, PIECE):
            size = min(PIECE, total - begin)
            near += jnp.dot(rows_ref[:, begin:begin + size], one_hot(index - begin, size),
                            preferred_element_type=jnp.float32)
        for c in range(chunks):
            near_ref[c, k] = near[:, c * LANES:(c + 1) * LANES]
        return carry

    lax.fori_loop(0, neigh, fetch, 0)

    def link(c, carry):
        lanes = pl.ds(pl.multiple_of(c * LANES, LANES), LANES)
        zero = jnp.zeros((8, LANES), jnp.float32)
        for k in range(neigh):
            mine = [near_ref[c, k, 8 * i:8 * i + 8, :] for i in range(2 * half)]
            for l in range(k, neigh):
                other = [near_ref[c, l, 8 * i:8 * i + 8, :] for i in range(2 * half)]
                real = mine[0] * other[0]
                for i in range(1, 2 * half):
                    real += mine[i] * other[i]
                gram_re[l, 8 * k:8 * k + 8, :] = real
                if l == k:
                    gram_im[l, 8 * k:8 * k + 8, :] = zero
                    continue
                imag = mine[0] * other[half]
                for i in range(1, half):
                    imag += mine[i] * other[half + i]
                back = mine[half] * other[0]
                for i in range(1, half):
                    back += mine[half + i] * other[i]
                imag = imag - back
                gram_re[k, 8 * l:8 * l + 8, :] = real
                gram_im[l, 8 * k:8 * k + 8, :] = imag
                gram_im[k, 8 * l:8 * l + 8, :] = -imag

        def column(ref, l):
            value = ref[l, pl.ds(0, neigh, stride=8), :]
            for j in range(1, 8):
                value += ref[l, pl.ds(j, neigh, stride=8), :]
            return value

        cols_re = [column(gram_re, l) for l in range(neigh)]
        cols_im = [column(gram_im, l) for l in range(neigh)]
        for l in range(neigh):
            gram_re[l, :neigh, :] = cols_re[l]
            gram_im[l, :neigh, :] = cols_im[l]
        mask = valid_ref[:, lanes].astype(jnp.float32)

        u_re = mask * gram_re[0, :neigh, :]
        u_im = mask * gram_im[0, :neigh, :]
        for turn in range(POWER_ITERS - 1):
            g_re = jnp.zeros((neigh, LANES), jnp.float32)
            g_im = jnp.zeros((neigh, LANES), jnp.float32)
            for l in range(neigh):
                a, b = gram_re[l, :neigh, :], gram_im[l, :neigh, :]
                x, y = u_re[l:l + 1, :], u_im[l:l + 1, :]
                g_re += a * x - b * y
                g_im += a * y + b * x
            power = jnp.sum(u_re * g_re + u_im * g_im, axis=0, keepdims=True)
            factor = lax.rsqrt(jnp.maximum(power, 0.0) / channels + eps)
            u_re = mask * g_re * factor
            u_im = mask * g_im * factor

        v_re = jnp.zeros((channels, LANES), jnp.float32)
        v_im = jnp.zeros((channels, LANES), jnp.float32)
        for k in range(neigh):
            a, b = near_ref[c, k, :channels, :], near_ref[c, k, channels:, :]
            x, y = u_re[k:k + 1, :], u_im[k:k + 1, :]
            v_re += a * x - b * y
            v_im += a * y + b * x
        power = jnp.sum(v_re * v_re + v_im * v_im, axis=0, keepdims=True)
        factor = lax.rsqrt(power / channels + eps)
        v_re = v_re * factor
        v_im = v_im * factor
        first_re, first_im = v_re[:1, :], v_im[:1, :]
        denom = jnp.maximum(jnp.sqrt(first_re * first_re + first_im * first_im), floor_value)
        scale_re, scale_im = first_re / denom, first_im / denom
        out_re = v_re * scale_re + v_im * scale_im
        out_im = v_im * scale_re - v_re * scale_im
        dates = out_ref.shape[2]
        for p in range(out_ref.shape[1]):
            out_ref[0, p, :, lanes] = out_re[p * dates:(p + 1) * dates, :]
            out_ref[1, p, :, lanes] = out_im[p * dates:(p + 1) * dates, :]
        return carry

    lax.fori_loop(0, chunks, link, 0)


def body(mesh, stack, nbr_tile, nbr_slot, nbr_valid, fetch_rows):
    dates, pols, tiles = mesh.shape["date"], mesh.shape["pol"], mesh.shape["tile"]
    strips = dates * pols
    parts, local, sets, span = stack.shape
    width = span // strips
    channels = strips * local * sets
    features = parts * channels
    capacity = fetch_rows.shape[-1]
    padded = -(-parts * sets * local // 16) * 16
    vmem = pl.BlockSpec(memory_space=pltpu.VMEM)
    table, fetched = pl.pallas_call(
        functools.partial(gather_kernel, dates, pols, tiles),
        out_shape=(jax.ShapeDtypeStruct((features, width), jnp.bfloat16),
                   jax.ShapeDtypeStruct((tiles, features, capacity), jnp.bfloat16)),
        in_specs=[vmem, vmem],
        out_specs=(vmem, vmem),
        scratch_shapes=[
            pltpu.VMEM((strips, padded, width), jnp.bfloat16),
            pltpu.VMEM((strips, padded, width), jnp.bfloat16),
            pltpu.VMEM((tiles, 1, capacity), jnp.int32),
            pltpu.VMEM((tiles, features, capacity), jnp.bfloat16),
            pltpu.SemaphoreType.DMA((strips,)),
            pltpu.SemaphoreType.DMA((strips,)),
            pltpu.SemaphoreType.DMA((tiles,)),
            pltpu.SemaphoreType.DMA((tiles,)),
            pltpu.SemaphoreType.DMA((tiles,)),
            pltpu.SemaphoreType.DMA((tiles,)),
        ],
        compiler_params=pltpu.CompilerParams(collective_id=0, has_side_effects=True,
                                             vmem_limit_bytes=32 << 20),
        name="gather_rows",
    )(jnp.transpose(stack, (0, 2, 1, 3)), fetch_rows.reshape(tiles, 1, capacity))

    neigh = nbr_tile.shape[0]
    home = lax.axis_index("tile").astype(jnp.int32).reshape(1)
    linked = pl.pallas_call(
        link_kernel,
        out_shape=jax.ShapeDtypeStruct((parts, sets, strips * local, width), jnp.float32),
        in_specs=[pl.BlockSpec(memory_space=pltpu.SMEM)] + [vmem] * 5,
        out_specs=vmem,
        scratch_shapes=[
            pltpu.VMEM((features, width + tiles * capacity), jnp.bfloat16),
            pltpu.VMEM((neigh, width), jnp.int32),
            pltpu.VMEM((width // LANES, neigh, features, LANES), jnp.float32),
            pltpu.VMEM((neigh, 8 * neigh, LANES), jnp.float32),
            pltpu.VMEM((neigh, 8 * neigh, LANES), jnp.float32),
        ],
        compiler_params=pltpu.CompilerParams(vmem_limit_bytes=48 << 20),
        name="link_phases",
    )(home, table, fetched, nbr_tile, nbr_slot, nbr_valid)
    return jnp.transpose(linked, (0, 2, 1, 3))


def solution(mesh):
    in_specs = (
        P(None, ("date", "pol"), None, ("grp", "tile")),
        P(None, ("grp", "tile", "date", "pol")),
        P(None, ("grp", "tile", "date", "pol")),
        P(None, ("grp", "tile", "date", "pol")),
        P(("grp", "tile"), ("date", "pol"), None, None),
    )
    out_specs = P(None, None, None, ("grp", "tile", "date", "pol"))
    return jax.shard_map(functools.partial(body, mesh), mesh=mesh, in_specs=in_specs, out_specs=out_specs,
                         check_vma=False)
```

time: 346 us -> 27.1 us (0.08)
  other arithmetic: 177 us -> 0 us
  local copies, waits for them, and re-layouts: 102 us -> 1.58 us
  matrix products: 36.4 us -> 0 us
  Pallas kernels: 0 us -> 25.3 us
  blocking collectives: 16.3 us -> 0 us
  loops' own time: 4.38 us -> 0 us
  starting transfers between devices: 4.23 us -> 0 us
  waiting for transfers between devices: 3.91 us -> 0 us
    while x28 -> x0, other arithmetic: 141 us -> none
    dot_general x8 -> x0, matrix products: 36.4 us -> none  [the longest x4 19.9 us: phase_link(): image = jnp.einsum('bij,bj->bi', operator, vector, precision=highest)]
    gather x5 -> x0, local copies, waits for them, and re-layouts: 26.1 us -> none  [the longest x4 24.7 us: link_block(): near = jnp.take(table, chosen, axis=0) * keep[:, :, None]]
    neg x4 -> x0, other arithmetic: 25.4 us -> none  [phase_link(): upper = jnp.concatenate([real_part, -imag_part], axis=2)]
    pallas_call x0 -> x2, Pallas kernels: none -> 25.3 us  [the longest x1 12.9 us: body(): pl.pallas_call(functools.partial(gather_kernel, dates, pols, tiles), out_...]
    while x76 -> x0, local copies, waits for them, and re-layouts: 23.9 us -> none
    all_gather x1 -> x0, blocking collectives: 16.3 us -> none  [body(): piece = lax.all_gather(rows_here, 'tile', axis=0, tiled=True)]
    unnamed x12 -> x10, local copies, waits for them, and re-layouts: 16.8 us -> 1.58 us
  transfers between devices with their start and end apart: 1 -> 0, of which waited for: 1 -> 0; matrix products, arithmetic and copies ran while one was open for 0% -> 0% of each run, Pallas kernels for 0% -> 0%
where the time goes in v1:
time: 27.1 us; the launch traced here: 26.9 us
  Pallas kernels  25.3 us (93%)
  local copies, waits for them, and re-layouts  1.58 us (6%)
    pallas_call x1, Pallas kernels, body(): pl.pallas_call(functools.partial(gather_kernel, dates, pols, tiles), out_...  12.9 us
    pallas_call x1, Pallas kernels, body(): pl.pallas_call(link_kernel, out_shape=jax.ShapeDtypeStruct((parts, sets,...  12.4 us
    unnamed x10, local copies, waits for them, and re-layouts  1.58 us

profile of v1, /device:TPU:0, one launch (start us, length us, event | category | flops | bytes accessed | tf_op | source)
XLA Modules:
  0.0 26.9 jit_solution(290017986162971139)
XLA Ops:
  0.0 0.0 copy-start.4
  0.0 0.7 %copy-done.4 = s32[1,1,4,128]{3,2,1,0:T(4,128)S(1)} copy-done((s32[1,1,4,128]{3,2,1,0:T(4,128)S(1)}, s32[1,1,4,128]{3,2,1,0:T(4,128)}, u32[]{:S(2)}) %copy-start.4) | copy-done | bytes 2072
  0.7 0.0 copy-start
  0.7 0.9 %copy-done = bf16[2,4,3,2048]{3,1,2,0:T(4,128)(2,1)S(1)} copy-done((bf16[2,4,3,2048]{3,1,2,0:T(4,128)(2,1)S(1)}, bf16[2,4,3,2048]{3,1,2,0:T(4,128)(2,1)}, u32[]{:S(2)}) %copy-start) | copy-done | bytes 98328
  1.6 0.0 copy-start.1
  1.6 0.0 copy-start.2
  1.6 0.0 copy-start.3
  1.6 12.9 %gather_rows.1 = (bf16[96,512]{1,0:T(8,128)(2,1)S(1)}, bf16[4,96,128]{2,1,0:T(8,128)(2,1)S(1)}) custom-call(bf16[2,3,4,2048]{3,2,1,0:T(4,128)(2,1)S(1)} %bitcast.4, s32[4,1,128]{2,1,0:T(1,128)S(1)} %bitcast.5), custom_call_target="tpu_custom_call" | custom-call | tf_op jit(solution)/shard_map/gather_rows/pallas_call | solution.py:219
  14.5 0.0 copy-done.1
  14.5 0.0 copy-done.2
  14.5 0.0 copy-done.3
  14.5 12.4 %link_phases.1 = f32[2,3,16,512]{3,2,1,0:T(8,128)} custom-call(s32[1]{0:T(128)} %bitcast.home_ref, bf16[96,512]{1,0:T(8,128)(2,1)S(1)} %get-tuple-element.7.table_ref, bf16[4,96,128]{2,1,0:T(8,128)(2,1)S(1)} %get-tuple-element.8.fetched_ref, s32[16,512]{1,0:T(8,128)S(1)} %copy-done.1, s32[16,512]{1,0:T(8,128)S(1)} %copy-done.2, s32[16,512]{1,0:T(8,128)S(1)} %copy-done.3), custom_call_target="tpu_custom_call" | custom-call | tf_op jit(solution)/shard_map/link_phases/pallas_call | solution.py:244
Async XLA Ops:
  0.0 0.7 %copy-start.4 = (s32[1,1,4,128]{3,2,1,0:T(4,128)S(1)}, s32[1,1,4,128]{3,2,1,0:T(4,128)}, u32[]{:S(2)}) copy-start(s32[1,1,4,128]{3,2,1,0:T(4,128)} %param.9) | copy-start | bytes 6148
  0.7 0.9 %copy-start = (bf16[2,4,3,2048]{3,1,2,0:T(4,128)(2,1)S(1)}, bf16[2,4,3,2048]{3,1,2,0:T(4,128)(2,1)}, u32[]{:S(2)}) copy-start(bf16[2,4,3,2048]{3,1,2,0:T(4,128)(2,1)} %param.5) | copy-start | bytes 294916
  1.6 12.9 %copy-start.1 = (s32[16,512]{1,0:T(8,128)S(1)}, s32[16,512]{1,0:T(8,128)}, u32[]{:S(2)}) copy-start(s32[16,512]{1,0:T(8,128)} %tile_ref.1) | copy-start | bytes 98308
  1.6 12.9 %copy-start.2 = (s32[16,512]{1,0:T(8,128)S(1)}, s32[16,512]{1,0:T(8,128)}, u32[]{:S(2)}) copy-start(s32[16,512]{1,0:T(8,128)} %slot_ref.1) | copy-start | bytes 98308
  1.6 12.9 %copy-start.3 = (s32[16,512]{1,0:T(8,128)S(1)}, s32[16,512]{1,0:T(8,128)}, u32[]{:S(2)}) copy-start(s32[16,512]{1,0:T(8,128)} %valid_ref.1) | copy-start | bytes 98308

commit v2 on v1

v2 whole, which is shorter than its diff:
```python
import functools

import jax
import jax.numpy as jnp
from jax import lax
from jax.experimental import pallas as pl
from jax.experimental.pallas import tpu as pltpu
from jax.sharding import PartitionSpec as P

POWER_ITERS = 8
LANES = 128
PIECE = 256
MESH = pl.DeviceIdType.MESH

eps = 1e-06
floor_value = 0.3


def one_hot(index, rows):
    pieces = []
    for begin in range(0, rows, PIECE):
        size = min(PIECE, rows - begin)
        row = lax.broadcasted_iota(jnp.int32, (size, LANES), 0).astype(jnp.float32).astype(jnp.bfloat16)
        near = (index - begin).astype(jnp.bfloat16)
        one, zero = jnp.ones((size, LANES), jnp.bfloat16), jnp.zeros((size, LANES), jnp.bfloat16)
        pieces.append(jnp.concatenate(
            [jnp.where(row == near[:, c:c + LANES], one, zero) for c in range(0, index.shape[1], LANES)], axis=1))
    return jnp.concatenate(pieces, axis=0)


def phase_kernel(dates, pols, tiles, stack_ref, wanted_ref, tile_ref, slot_ref, valid_ref, out_ref,
                  near_ref, sum_re, sum_im, gram_re, gram_im, last_re, last_im, valid_here, inbox, asked, picked, fetched, table_ref, tile_here, slot_here, source_ref, hot_pick, hot_own, hot_far,
                  own_sem, out_sem, in_sem, ask_sem, asked_sem, pick_sem, fetch_sem):
    strips = dates * pols
    parts, sets, local, _ = stack_ref.shape
    features, width = table_ref.shape
    neigh = tile_ref.shape[0]
    capacity = wanted_ref.shape[-1]
    chunks = width // LANES
    date, pol, tile = lax.axis_index("date"), lax.axis_index("pol"), lax.axis_index("tile")
    me = date * pols + pol

    barrier = pltpu.get_barrier_semaphore()
    for step in range(1, strips):
        peer = lax.rem(me + step, strips)
        pl.semaphore_signal(barrier, inc=1, device_id={"date": peer // pols, "pol": lax.rem(peer, pols)},
                            device_id_type=MESH)
    for step in range(1, tiles):
        pl.semaphore_signal(barrier, inc=1, device_id={"tile": lax.rem(tile + step, tiles)}, device_id_type=MESH)

    def part(strip):
        return stack_ref.at[:, :, :, pl.ds(pl.multiple_of(strip * width, LANES), width)]

    keep = [pltpu.make_async_copy(part(me), inbox.at[me], own_sem.at[0]),
            pltpu.make_async_copy(tile_ref, tile_here, own_sem.at[1]),
            pltpu.make_async_copy(slot_ref, slot_here, own_sem.at[2]),
            pltpu.make_async_copy(valid_ref, valid_here, own_sem.at[3])]
    for copy in keep:
        copy.start()
    fetched[tile] = jnp.zeros(fetched.shape[1:], jnp.bfloat16)

    pl.semaphore_wait(barrier, strips - 1 + tiles - 1)

    asks = []
    for step in range(1, tiles):
        peer = lax.rem(tile + step, tiles)
        copy = pltpu.make_async_remote_copy(
            src_ref=wanted_ref.at[peer], dst_ref=asked.at[step],
            send_sem=ask_sem.at[step], recv_sem=asked_sem.at[step],
            device_id={"tile": peer}, device_id_type=MESH)
        copy.start()
        asks.append(copy)
    sends = []
    for step in range(1, strips):
        peer = lax.rem(me + step, strips)
        copy = pltpu.make_async_remote_copy(
            src_ref=part(peer), dst_ref=inbox.at[me],
            send_sem=out_sem.at[step], recv_sem=in_sem.at[step],
            device_id={"date": peer // pols, "pol": lax.rem(peer, pols)}, device_id_type=MESH)
        copy.start()
        sends.append(copy)

    for copy in keep:
        copy.wait()
    owner, slot = tile_here[...], slot_here[...]
    source_ref[...] = jnp.where(owner == tile, slot, width + owner * capacity + slot).astype(jnp.float32)

    def prepare(k, carry):
        hot_own[k] = one_hot(source_ref[pl.ds(k, 1), :], width)
        return carry

    lax.fori_loop(0, neigh, prepare, 0)
    for step in range(1, tiles):
        asks[step - 1].wait_recv()
        hot_pick[step] = one_hot(asked[step].astype(jnp.float32), width)
    for copy in sends:
        copy.wait_recv()

    pieces = []
    for r in range(parts):
        for p in range(sets):
            for s in range(strips):
                pieces.append(inbox[s, r, p].astype(jnp.float32))
    table_ref[...] = jnp.concatenate(pieces, axis=0).astype(jnp.bfloat16)

    picks = []
    for step in range(1, tiles):
        asker = lax.rem(tile + tiles - step, tiles)
        picked[step] = jnp.dot(table_ref[...], hot_pick[step], preferred_element_type=jnp.float32).astype(jnp.bfloat16)
        copy = pltpu.make_async_remote_copy(
            src_ref=picked.at[step], dst_ref=fetched.at[tile],
            send_sem=pick_sem.at[step], recv_sem=fetch_sem.at[step],
            device_id={"tile": asker}, device_id_type=MESH)
        copy.start()
        picks.append(copy)

    far = tiles * capacity
    early = hot_far.shape[1] == far

    def gather_own(k, carry):
        if early:
            hot_far[k] = one_hot(source_ref[pl.ds(k, 1), :] - width, far)
        near = jnp.dot(table_ref[...], hot_own[k], preferred_element_type=jnp.float32)
        for c in range(chunks):
            near_ref[c, k] = near[:, c * LANES:(c + 1) * LANES]
        return carry

    lax.fori_loop(0, neigh, gather_own, 0)
    for copy in picks:
        copy.wait_recv()

    def gather_far(k, carry):
        group = max(1, 2 * PIECE // capacity)
        near = jnp.zeros((features, width), jnp.float32)
        for begin in range(0, tiles, group):
            end = min(tiles, begin + group)
            rows = jnp.concatenate([fetched[q] for q in range(begin, end)], axis=1)
            first, size = begin * capacity, (end - begin) * capacity
            if early:
                hot = hot_far[k, first:first + size, :]
            else:
                hot = one_hot(source_ref[pl.ds(k, 1), :] - (width + first), size)
            near += jnp.dot(rows, hot, preferred_element_type=jnp.float32)
        for c in range(chunks):
            near_ref[c, k] += near[:, c * LANES:(c + 1) * LANES]
        return carry

    group = next(n for n in (4, 4, 2, 1) if neigh % n == 0)

    def gather_group(i, carry):
        for j in range(group):
            carry = gather_far(i * group + j, carry)
        return carry

    lax.fori_loop(0, neigh // group, gather_group, 0)
    link_rows(near_ref, valid_here, out_ref, sum_re, sum_im, gram_re, gram_im, last_re, last_im)
    for copy in asks + sends + picks:
        copy.wait_send()


def link_rows(near_ref, valid_ref, out_ref, sum_re, sum_im, gram_re, gram_im, last_re, last_im):
    chunks, neigh, features, _ = near_ref.shape
    channels = features // 2
    half = channels // 8

    def pairs(c, carry):
        lanes = pl.ds(pl.multiple_of(c * LANES, LANES), LANES)
        zero = jnp.zeros((8, LANES), jnp.float32)
        for k in range(neigh):
            mine = [near_ref[c, k, 8 * i:8 * i + 8, :] for i in range(2 * half)]
            for l in range(k, neigh):
                other = [near_ref[c, l, 8 * i:8 * i + 8, :] for i in range(2 * half)]
                real = mine[0] * other[0]
                for i in range(1, 2 * half):
                    real += mine[i] * other[i]
                sum_re[l, 8 * k:8 * k + 8, :] = real
                if l == k:
                    sum_im[l, 8 * k:8 * k + 8, :] = zero
                    continue
                imag = mine[0] * other[half]
                for i in range(1, half):
                    imag += mine[i] * other[half + i]
                back = mine[half] * other[0]
                for i in range(1, half):
                    back += mine[half + i] * other[i]
                imag = imag - back
                sum_re[k, 8 * l:8 * l + 8, :] = real
                sum_im[l, 8 * k:8 * k + 8, :] = imag
                sum_im[k, 8 * l:8 * l + 8, :] = -imag
        for l in range(neigh):
            for held, gram in ((sum_re, gram_re), (sum_im, gram_im)):
                value = held[l, pl.ds(0, neigh, stride=8), :]
                for j in range(1, 8):
                    value += held[l, pl.ds(j, neigh, stride=8), :]
                gram[l, :, lanes] = value
        return carry

    lax.fori_loop(0, chunks, pairs, 0)

    mask = valid_ref[...].astype(jnp.float32)
    u_re = mask * gram_re[0]
    u_im = mask * gram_im[0]
    for turn in range(POWER_ITERS - 1):
        g_re = jnp.zeros(mask.shape, jnp.float32)
        g_im = jnp.zeros(mask.shape, jnp.float32)
        for l in range(neigh):
            a, b = gram_re[l], gram_im[l]
            x, y = u_re[l:l + 1, :], u_im[l:l + 1, :]
            g_re += a * x - b * y
            g_im += a * y + b * x
        power = jnp.sum(u_re * g_re + u_im * g_im, axis=0, keepdims=True)
        factor = lax.rsqrt(jnp.maximum(power, 0.0) / channels + eps)
        u_re = mask * g_re * factor
        u_im = mask * g_im * factor
    last_re[...] = u_re
    last_im[...] = u_im

    dates = out_ref.shape[2]
    for c in range(chunks):
        lanes = slice(c * LANES, (c + 1) * LANES)
        v_re = jnp.zeros((channels, LANES), jnp.float32)
        v_im = jnp.zeros((channels, LANES), jnp.float32)
        for k in range(neigh):
            a, b = near_ref[c, k, :channels, :], near_ref[c, k, channels:, :]
            x, y = last_re[k:k + 1, lanes], last_im[k:k + 1, lanes]
            v_re += a * x - b * y
            v_im += a * y + b * x
        power = jnp.sum(v_re * v_re + v_im * v_im, axis=0, keepdims=True)
        factor = lax.rsqrt(power / channels + eps)
        v_re = v_re * factor
        v_im = v_im * factor
        first_re, first_im = v_re[:1, :], v_im[:1, :]
        denom = jnp.maximum(jnp.sqrt(first_re * first_re + first_im * first_im), floor_value)
        scale_re, scale_im = first_re / denom, first_im / denom
        out_re = v_re * scale_re + v_im * scale_im
        out_im = v_im * scale_re - v_re * scale_im
        for p in range(out_ref.shape[1]):
            out_ref[0, p, :, lanes] = out_re[p * dates:(p + 1) * dates, :]
            out_ref[1, p, :, lanes] = out_im[p * dates:(p + 1) * dates, :]


def body(mesh, stack, nbr_tile, nbr_slot, nbr_valid, fetch_rows):
    dates, pols, tiles = mesh.shape["date"], mesh.shape["pol"], mesh.shape["tile"]
    strips = dates * pols
    parts, local, sets, span = stack.shape
    width = span // strips
    features = parts * strips * local * sets
    capacity = fetch_rows.shape[-1]
    neigh = nbr_tile.shape[0]
    far = tiles * capacity if tiles * capacity <= 1024 else 16
    vmem = pl.BlockSpec(memory_space=pltpu.VMEM)
    anywhere = pl.BlockSpec(memory_space=pl.ANY)
    linked = pl.pallas_call(
        functools.partial(phase_kernel, dates, pols, tiles),
        out_shape=jax.ShapeDtypeStruct((parts, sets, strips * local, width), jnp.float32),
        in_specs=[anywhere] * 5,
        out_specs=vmem,
        scratch_shapes=[
            pltpu.VMEM((width // LANES, neigh, features, LANES), jnp.float32),
            pltpu.VMEM((neigh, 8 * neigh, LANES), jnp.float32),
            pltpu.VMEM((neigh, 8 * neigh, LANES), jnp.float32),
            pltpu.VMEM((neigh, neigh, width), jnp.float32),
            pltpu.VMEM((neigh, neigh, width), jnp.float32),
            pltpu.VMEM((neigh, width), jnp.float32),
            pltpu.VMEM((neigh, width), jnp.float32),
            pltpu.VMEM((neigh, width), jnp.int32),
            pltpu.VMEM((strips, parts, sets, local, width), jnp.bfloat16),
            pltpu.VMEM((tiles, 1, capacity), jnp.int32),
            pltpu.VMEM((tiles, features, capacity), jnp.bfloat16),
            pltpu.VMEM((tiles, features, capacity), jnp.bfloat16),
            pltpu.VMEM((features, width), jnp.bfloat16),
            pltpu.VMEM((neigh, width), jnp.int32),
            pltpu.VMEM((neigh, width), jnp.int32),
            pltpu.VMEM((neigh, width), jnp.float32),
            pltpu.VMEM((tiles, width, capacity), jnp.bfloat16),
            pltpu.VMEM((neigh, width, width), jnp.bfloat16),
            pltpu.VMEM((neigh, far, width), jnp.bfloat16),
            pltpu.SemaphoreType.DMA((4,)),
            pltpu.SemaphoreType.DMA((strips,)),
            pltpu.SemaphoreType.DMA((strips,)),
            pltpu.SemaphoreType.DMA((tiles,)),
            pltpu.SemaphoreType.DMA((tiles,)),
            pltpu.SemaphoreType.DMA((tiles,)),
            pltpu.SemaphoreType.DMA((tiles,)),
        ],
        compiler_params=pltpu.CompilerParams(collective_id=0, has_side_effects=True,
                                             vmem_limit_bytes=60 << 20),
        name="phase_rows",
    )(jnp.transpose(stack, (0, 2, 1, 3)), fetch_rows.reshape(tiles, 1, capacity), nbr_tile, nbr_slot, nbr_valid)

    return jnp.transpose(linked, (0, 2, 1, 3))


def solution(mesh):
    in_specs = (
        P(None, ("date", "pol"), None, ("grp", "tile")),
        P(None, ("grp", "tile", "date", "pol")),
        P(None, ("grp", "tile", "date", "pol")),
        P(None, ("grp", "tile", "date", "pol")),
        P(("grp", "tile"), ("date", "pol"), None, None),
    )
    out_specs = P(None, None, None, ("grp", "tile", "date", "pol"))
    return jax.shard_map(functools.partial(body, mesh), mesh=mesh, in_specs=in_specs, out_specs=out_specs,
                         check_vma=False)
```

time: 27.1 us -> 24.2 us (0.89)
  Pallas kernels: 25.3 us -> 22.4 us
    pallas_call x2 -> x1, Pallas kernels: 25.3 us -> 22.4 us  [body(): pl.pallas_call(functools.partial(phase_kernel, dates, pols, tiles), out_s...]
    unnamed x10 -> x1, local copies, waits for them, and re-layouts: 1.58 us -> 1.62 us
where the time goes in v2:
time: 24.2 us; the launch traced here: 24 us
  Pallas kernels  22.4 us (93%)
  local copies, waits for them, and re-layouts  1.62 us (7%)
    pallas_call x1, Pallas kernels, body(): pl.pallas_call(functools.partial(phase_kernel, dates, pols, tiles), out_s...  22.4 us
    unnamed x1, local copies, waits for them, and re-layouts  1.62 us

profile of v2, /device:TPU:0, one launch (start us, length us, event | category | flops | bytes accessed | tf_op | source)
XLA Modules:
  0.0 24.0 jit_solution(3775859264165463429)
XLA Ops:
  0.0 22.4 %phase_rows.1 = f32[2,3,16,512]{3,2,1,0:T(8,128)} custom-call(bf16[2,3,4,2048]{3,2,1,0:T(4,128)(2,1)} %bitcast.4, s32[4,1,128]{2,1,0:T(1,128)} %bitcast.5, s32[16,512]{1,0:T(8,128)} %tile_ref.1, s32[16,512]{1,0:T(8,128)} %slot_ref.1, s32[16,512]{1,0:T(8,128)} %valid_ref.1), custom_call_target="tpu_custom_call" | custom-call | tf_op jit(solution)/shard_map/phase_rows/pallas_call | solution.py:253
  22.4 1.6 %copy.7 = f32[2,16,3,512]{3,1,2,0:T(8,128)} copy(f32[2,16,3,512]{3,1,2,0:T(8,128)} %bitcast.3) | data formatting | bytes 393216

commit v3 on v2

--- a/solution.py
+++ b/solution.py
@@ -29,7 +29,7 @@
 
 
 def phase_kernel(dates, pols, tiles, stack_ref, wanted_ref, tile_ref, slot_ref, valid_ref, out_ref,
-                  near_ref, sum_re, sum_im, gram_re, gram_im, last_re, last_im, valid_here, inbox, asked, picked, fetched, table_ref, tile_here, slot_here, source_ref, hot_pick, hot_own, hot_far,
+                  near_ref, diff_ref, sum_re, sum_im, gram_re, gram_im, last_re, last_im, valid_here, inbox, asked, picked, fetched, table_ref, tile_here, slot_here, source_ref, hot_pick, hot_own, hot_far,
                   own_sem, out_sem, in_sem, ask_sem, asked_sem, pick_sem, fetch_sem):
     strips = dates * pols
     parts, sets, local, _ = stack_ref.shape
@@ -103,10 +103,11 @@
                 pieces.append(inbox[s, r, p].astype(jnp.float32))
     table_ref[...] = jnp.concatenate(pieces, axis=0).astype(jnp.bfloat16)
 
+    for step in range(1, tiles):
+        picked[step] = jnp.dot(table_ref[...], hot_pick[step], preferred_element_type=jnp.float32).astype(jnp.bfloat16)
     picks = []
     for step in range(1, tiles):
         asker = lax.rem(tile + tiles - step, tiles)
-        picked[step] = jnp.dot(table_ref[...], hot_pick[step], preferred_element_type=jnp.float32).astype(jnp.bfloat16)
         copy = pltpu.make_async_remote_copy(
             src_ref=picked.at[step], dst_ref=fetched.at[tile],
             send_sem=pick_sem.at[step], recv_sem=fetch_sem.at[step],
@@ -125,7 +126,14 @@
             near_ref[c, k] = near[:, c * LANES:(c + 1) * LANES]
         return carry
 
-    lax.fori_loop(0, neigh, gather_own, 0)
+    group = next(n for n in (4, 2, 1) if neigh % n == 0)
+
+    def own_group(i, carry):
+        for j in range(group):
+            carry = gather_own(i * group + j, carry)
+        return carry
+
+    lax.fori_loop(0, neigh // group, own_group, 0)
     for copy in picks:
         copy.wait_recv()
 
@@ -134,18 +142,18 @@
         near = jnp.zeros((features, width), jnp.float32)
         for begin in range(0, tiles, group):
             end = min(tiles, begin + group)
-            rows = jnp.concatenate([fetched[q] for q in range(begin, end)], axis=1)
+            block = jnp.concatenate([fetched[q] for q in range(begin, end)], axis=1)
             first, size = begin * capacity, (end - begin) * capacity
             if early:
                 hot = hot_far[k, first:first + size, :]
             else:
                 hot = one_hot(source_ref[pl.ds(k, 1), :] - (width + first), size)
-            near += jnp.dot(rows, hot, preferred_element_type=jnp.float32)
+            near += jnp.dot(block, hot, preferred_element_type=jnp.float32)
         for c in range(chunks):
-            near_ref[c, k] += near[:, c * LANES:(c + 1) * LANES]
-        return carry
-
-    group = next(n for n in (4, 4, 2, 1) if neigh % n == 0)
+            rows = near_ref[c, k] + near[:, c * LANES:(c + 1) * LANES]
+            near_ref[c, k] = rows
+            diff_ref[c, k] = rows[:features // 2] - rows[features // 2:]
+        return carry
 
     def gather_group(i, carry):
         for j in range(group):
@@ -153,12 +161,12 @@
         return carry
 
     lax.fori_loop(0, neigh // group, gather_group, 0)
-    link_rows(near_ref, valid_here, out_ref, sum_re, sum_im, gram_re, gram_im, last_re, last_im)
+    link_rows(near_ref, diff_ref, valid_here, out_ref, sum_re, sum_im, gram_re, gram_im, last_re, last_im)
     for copy in asks + sends + picks:
         copy.wait_send()
 
 
-def link_rows(near_ref, valid_ref, out_ref, sum_re, sum_im, gram_re, gram_im, last_re, last_im):
+def link_rows(near_ref, diff_ref, valid_ref, out_ref, sum_re, sum_im, gram_re, gram_im, last_re, last_im):
     chunks, neigh, features, _ = near_ref.shape
     channels = features // 2
     half = channels // 8
@@ -168,22 +176,23 @@
         zero = jnp.zeros((8, LANES), jnp.float32)
         for k in range(neigh):
             mine = [near_ref[c, k, 8 * i:8 * i + 8, :] for i in range(2 * half)]
+            both = [mine[i] + mine[half + i] for i in range(half)]
             for l in range(k, neigh):
                 other = [near_ref[c, l, 8 * i:8 * i + 8, :] for i in range(2 * half)]
-                real = mine[0] * other[0]
-                for i in range(1, 2 * half):
-                    real += mine[i] * other[i]
+                first = mine[0] * other[0]
+                second = mine[half] * other[half]
+                for i in range(1, half):
+                    first += mine[i] * other[i]
+                    second += mine[half + i] * other[half + i]
+                real = first + second
                 sum_re[l, 8 * k:8 * k + 8, :] = real
                 if l == k:
                     sum_im[l, 8 * k:8 * k + 8, :] = zero
                     continue
-                imag = mine[0] * other[half]
+                third = both[0] * diff_ref[c, l, :8, :]
                 for i in range(1, half):
-                    imag += mine[i] * other[half + i]
-                back = mine[half] * other[0]
-                for i in range(1, half):
-                    back += mine[half + i] * other[i]
-                imag = imag - back
+                    third += both[i] * diff_ref[c, l, 8 * i:8 * i + 8, :]
+                imag = first - second - third
                 sum_re[k, 8 * l:8 * l + 8, :] = real
                 sum_im[l, 8 * k:8 * k + 8, :] = imag
                 sum_im[k, 8 * l:8 * l + 8, :] = -imag
@@ -257,6 +266,7 @@
         out_specs=vmem,
         scratch_shapes=[
             pltpu.VMEM((width // LANES, neigh, features, LANES), jnp.float32),
+            pltpu.VMEM((width // LANES, neigh, features // 2, LANES), jnp.float32),
             pltpu.VMEM((neigh, 8 * neigh, LANES), jnp.float32),
             pltpu.VMEM((neigh, 8 * neigh, LANES), jnp.float32),
             pltpu.VMEM((neigh, neigh, width), jnp.float32),

time: 24.2 us -> 23.4 us (0.967)
  Pallas kernels: 22.4 us -> 21.7 us
    pallas_call x1, Pallas kernels: 22.4 us -> 21.7 us  [body(): pl.pallas_call(functools.partial(phase_kernel, dates, pols, tiles), out_s...]
where the time goes in v3:
time: 23.4 us; the launch traced here: 23.3 us
  Pallas kernels  21.7 us (93%)
  local copies, waits for them, and re-layouts  1.62 us (7%)
    pallas_call x1, Pallas kernels, body(): pl.pallas_call(functools.partial(phase_kernel, dates, pols, tiles), out_s...  21.7 us
    unnamed x1, local copies, waits for them, and re-layouts  1.62 us

profile of v3, /device:TPU:0, one launch (start us, length us, event | category | flops | bytes accessed | tf_op | source)
XLA Modules:
  0.0 23.3 jit_solution(17940784139798272420)
XLA Ops:
  0.0 21.7 %phase_rows.1 = f32[2,3,16,512]{3,2,1,0:T(8,128)} custom-call(bf16[2,3,4,2048]{3,2,1,0:T(4,128)(2,1)} %bitcast.4, s32[4,1,128]{2,1,0:T(1,128)} %bitcast.5, s32[16,512]{1,0:T(8,128)} %tile_ref.1, s32[16,512]{1,0:T(8,128)} %slot_ref.1, s32[16,512]{1,0:T(8,128)} %valid_ref.1), custom_call_target="tpu_custom_call" | custom-call | tf_op jit(solution)/shard_map/phase_rows/pallas_call | solution.py:262
  21.7 1.6 %copy.7 = f32[2,16,3,512]{3,1,2,0:T(8,128)} copy(f32[2,16,3,512]{3,1,2,0:T(8,128)} %bitcast.3) | data formatting | bytes 393216

commit v4 on v3

--- a/solution.py
+++ b/solution.py
@@ -61,15 +61,6 @@
 
     pl.semaphore_wait(barrier, strips - 1 + tiles - 1)
 
-    asks = []
-    for step in range(1, tiles):
-        peer = lax.rem(tile + step, tiles)
-        copy = pltpu.make_async_remote_copy(
-            src_ref=wanted_ref.at[peer], dst_ref=asked.at[step],
-            send_sem=ask_sem.at[step], recv_sem=asked_sem.at[step],
-            device_id={"tile": peer}, device_id_type=MESH)
-        copy.start()
-        asks.append(copy)
     sends = []
     for step in range(1, strips):
         peer = lax.rem(me + step, strips)
@@ -79,7 +70,15 @@
             device_id={"date": peer // pols, "pol": lax.rem(peer, pols)}, device_id_type=MESH)
         copy.start()
         sends.append(copy)
-
+    asks = []
+    for step in range(1, tiles):
+        peer = lax.rem(tile + step, tiles)
+        copy = pltpu.make_async_remote_copy(
+            src_ref=wanted_ref.at[peer], dst_ref=asked.at[step],
+            send_sem=ask_sem.at[step], recv_sem=asked_sem.at[step],
+            device_id={"tile": peer}, device_id_type=MESH)
+        copy.start()
+        asks.append(copy)
     for copy in keep:
         copy.wait()
     owner, slot = tile_here[...], slot_here[...]
@@ -126,7 +125,7 @@
             near_ref[c, k] = near[:, c * LANES:(c + 1) * LANES]
         return carry
 
-    group = next(n for n in (4, 2, 1) if neigh % n == 0)
+    group = next(n for n in (8, 4, 2, 1) if neigh % n == 0)
 
     def own_group(i, carry):
         for j in range(group):

time: 23.4 us -> 23.2 us (level)
  Pallas kernels: 21.7 us -> 21.4 us
    pallas_call x1, Pallas kernels: 21.7 us -> 21.4 us  [body(): pl.pallas_call(functools.partial(phase_kernel, dates, pols, tiles), out_s...]
where the time goes in v4:
time: 23.2 us; the launch traced here: 23 us
  Pallas kernels  21.4 us (92%)
  local copies, waits for them, and re-layouts  1.62 us (7%)
    pallas_call x1, Pallas kernels, body(): pl.pallas_call(functools.partial(phase_kernel, dates, pols, tiles), out_s...  21.4 us
    unnamed x1, local copies, waits for them, and re-layouts  1.62 us

profile of v4, /device:TPU:0, one launch (start us, length us, event | category | flops | bytes accessed | tf_op | source)
XLA Modules:
  0.0 23.0 jit_solution(10825187607422017229)
XLA Ops:
  0.0 21.4 %phase_rows.1 = f32[2,3,16,512]{3,2,1,0:T(8,128)} custom-call(bf16[2,3,4,2048]{3,2,1,0:T(4,128)(2,1)} %bitcast.4, s32[4,1,128]{2,1,0:T(1,128)} %bitcast.5, s32[16,512]{1,0:T(8,128)} %tile_ref.1, s32[16,512]{1,0:T(8,128)} %slot_ref.1, s32[16,512]{1,0:T(8,128)} %valid_ref.1), custom_call_target="tpu_custom_call" | custom-call | tf_op jit(solution)/shard_map/phase_rows/pallas_call | solution.py:261
  21.4 1.6 %copy.7 = f32[2,16,3,512]{3,1,2,0:T(8,128)} copy(f32[2,16,3,512]{3,1,2,0:T(8,128)} %bitcast.3) | data formatting | bytes 393216
